TPU v7x, 32 devices: a whole 2x2x4 slice. The times are simulated.
32 devices in a mesh: dp: 8 (over y, x, core), fsdp: 4 (over z).
Axes of the slice: x: 2, y: 2, z: 4, core: 2. Of those that a mesh axis runs over, the one named last changes fastest.
Arguments:
- rollout_rows: bfloat16 [4096, 8192], P(('dp', 'fsdp')), may hold values from -6 to 6
- lengths: int32 [32, 8], P(('dp', 'fsdp')), may hold values from 1 to 32, as said below
- dest: int32 [32, 8], P(('dp', 'fsdp')), may hold values from 0 to 7, as said below
- offset: int32 [32, 8], P(('dp', 'fsdp')), may hold values from 0 to 96, as said below
- query: bfloat16 [4096, 4096], P(('dp', 'fsdp')), may hold values from -100 to 100
- key_rows: bfloat16 [4096, 512], P(('dp', 'fsdp')), may hold values from -5 to 5
- value_weight: bfloat16 [8192, 512], P('fsdp'), may hold values from -0.0625 to 0.0625
- d_out: bfloat16 [4096, 4096], P(('dp', 'fsdp')), may hold values from -6 to 6
Outputs:
- attn_out: bfloat16 [4096, 4096], P(('dp', 'fsdp'))
- grad_query: bfloat16 [4096, 4096], P(('dp', 'fsdp'))
- grad_key: bfloat16 [4096, 512], P(('dp', 'fsdp'))
- grad_input: bfloat16 [4096, 8192], P(('dp', 'fsdp'))
- grad_weight: float32 [8192, 512], P(('dp', 'fsdp'))
Inputs may be any that keep to these rules, and one draw needn't show every extreme that they name: Each rollout device's 8 lengths sum to 128. `dest`: the learner has the sender's fsdp index; the sequences of one device go to 8 different learner devices. `offset`: the sequences that a learner device receives cover its 128 rows exactly once; on every learner device the last of them is one of 32 rows.
All inputs are finite; a program needn't handle non-finite values.
Results may differ from a plain program's by a relative error of at most 0.006.
Values may be sent and summed in bfloat16 or wider, within the bound.
A program may use at most 128 MiB of HBM per device.

v0:
```python
import math
import jax
import jax.numpy as jnp
from jax import lax
from jax.sharding import PartitionSpec as P

HEAD_SIZE = 128
QUERY_HEADS = 32
KEY_VALUE_HEADS = 4


def attend(block_queries, block_keys, block_values, segment, gradient_block):
    row_count_total = block_queries.shape[0]
    share_ratio = QUERY_HEADS // KEY_VALUE_HEADS
    score_scale = 1.0 / math.sqrt(HEAD_SIZE)
    heads_queries = block_queries.reshape(row_count_total, KEY_VALUE_HEADS, share_ratio, HEAD_SIZE)
    heads_keys = block_keys.reshape(row_count_total, KEY_VALUE_HEADS, HEAD_SIZE)
    heads_values = block_values.reshape(row_count_total, KEY_VALUE_HEADS, HEAD_SIZE)
    gradient_heads = gradient_block.reshape(
        row_count_total, KEY_VALUE_HEADS, share_ratio, HEAD_SIZE
    )
    logit_scores = (
        jnp.einsum("euaz,nuz->uaen", heads_queries, heads_keys, preferred_element_type=jnp.float32)
        * score_scale
    )
    position = jnp.arange(row_count_total, dtype=jnp.int32)
    allowed = (segment[:, None] == segment[None, :]) & (position[None, :] <= position[:, None])
    logit_scores = jnp.where(allowed, logit_scores, -1e30)
    highest = jnp.max(logit_scores, axis=-1, keepdims=True)
    expo = jnp.exp(logit_scores - highest)
    probs = expo / jnp.sum(expo, axis=-1, keepdims=True)
    probs_reduced = probs.astype(jnp.bfloat16)
    attention_output = jnp.einsum(
        "yxmd,dya->myxa", probs_reduced, heads_values, preferred_element_type=jnp.float32
    )
    attention_output = attention_output.reshape(row_count_total, QUERY_HEADS * HEAD_SIZE).astype(
        jnp.bfloat16
    )
    gradient_probs = jnp.einsum(
        "euaz,nuz->uaen", gradient_heads, heads_values, preferred_element_type=jnp.float32
    )
    value_gradient = jnp.einsum(
        "lbjm,jlbw->mlw", probs_reduced, gradient_heads, preferred_element_type=jnp.float32
    )
    value_gradient = value_gradient.reshape(row_count_total, KEY_VALUE_HEADS * HEAD_SIZE).astype(
        jnp.bfloat16
    )
    inner = jnp.sum(probs * gradient_probs, axis=-1, keepdims=True)
    gradient_scores = (probs * (gradient_probs - inner) * score_scale).astype(jnp.bfloat16)
    query_gradient = jnp.einsum(
        "yxmd,dya->myxa", gradient_scores, heads_keys, preferred_element_type=jnp.float32
    )
    key_gradient = jnp.einsum(
        "lbjm,jlbw->mlw", gradient_scores, heads_queries, preferred_element_type=jnp.float32
    )
    return (
        attention_output,
        query_gradient.reshape(row_count_total, QUERY_HEADS * HEAD_SIZE).astype(jnp.bfloat16),
        key_gradient.reshape(row_count_total, KEY_VALUE_HEADS * HEAD_SIZE).astype(jnp.bfloat16),
        value_gradient,
    )


def tables(plan, tok_rows):
    seq_len, dest, offset = (plan[:, 0], plan[:, 1], plan[:, 2])
    order = jnp.arange(seq_len.shape[1], dtype=jnp.int32)
    earlier = order[None, :] < order[:, None]
    starts = jnp.sum(jnp.where(earlier[None], seq_len[:, None, :], 0), axis=2)
    rows = jnp.arange(tok_rows, dtype=jnp.int32)[None, :, None]
    inside = (rows >= starts[:, None, :]) & (rows < (starts + seq_len)[:, None, :])
    landing = (dest * tok_rows + offset - starts)[:, None, :] + rows
    return jnp.sum(jnp.where(inside, landing, 0), axis=2).reshape(-1)


def senders(plan, me, tok_rows):
    seq_len, dest, offset = (plan[:, 0], plan[:, 1], plan[:, 2])
    mine = dest == me
    land_off = jnp.sum(jnp.where(mine, offset, 0), axis=1)
    land_len = jnp.sum(jnp.where(mine, seq_len, 0), axis=1)
    rows = jnp.arange(tok_rows, dtype=jnp.int32)[:, None]
    inside = (rows >= land_off[None, :]) & (rows < (land_off + land_len)[None, :])
    source = jnp.arange(plan.shape[0], dtype=jnp.int32)
    return jnp.sum(jnp.where(inside, source[None, :], 0), axis=1)


def local(rollout_rows, lengths, dest, offset, query, key_rows, value_weight, d_out):
    n_dp = lax.axis_size("dp")
    n_fsdp = lax.axis_size("fsdp")
    me = lax.axis_index("dp")
    tok_rows = rollout_rows.shape[0]
    column = tok_rows * n_dp
    plan = lax.all_gather(jnp.concatenate([lengths, dest, offset], axis=0), "dp", axis=0)
    shared = lax.all_to_all(rollout_rows, "dp", split_axis=1, concat_axis=0, tiled=True)
    block = value_weight.shape[0] // n_dp
    piece = lax.dynamic_slice_in_dim(value_weight, me * block, block, axis=0)
    pairs = [(a * n_fsdp + b, b * n_dp + a) for a in range(n_dp) for b in range(n_fsdp)]
    piece = lax.ppermute(piece, ("dp", "fsdp"), pairs)
    weight = lax.all_gather(piece, "fsdp", axis=0, tiled=True)
    landing = tables(plan, tok_rows)
    pick = (jnp.arange(column, dtype=jnp.int32)[:, None] == landing[None, :]).astype(jnp.bfloat16)
    rows = jnp.dot(pick, shared, preferred_element_type=jnp.float32).astype(jnp.bfloat16)
    partial = jnp.dot(rows, weight, preferred_element_type=jnp.float32).astype(jnp.bfloat16)
    parts = lax.all_to_all(
        partial.reshape(n_dp, tok_rows, partial.shape[1]),
        "dp",
        split_axis=0,
        concat_axis=0,
        tiled=True,
    )
    values = jnp.sum(parts.astype(jnp.float32), axis=0).astype(jnp.bfloat16)
    attention_output, query_gradient, key_gradient, value_gradient = attend(
        query, key_rows, values, senders(plan, me, tok_rows), d_out
    )
    gathered = lax.all_gather(value_gradient, "dp", axis=0, tiled=True)
    grad_weight = lax.psum_scatter(
        lax.dot_general(
            rows, gathered, (((0,), (0,)), ((), ())), preferred_element_type=jnp.float32
        ),
        "fsdp",
        scatter_dimension=0,
        tiled=True,
    )
    grad_weight = grad_weight * (1.0 / math.sqrt(column * n_fsdp))
    share = lax.dot_general(
        gathered, weight, (((1,), (1,)), ((), ())), preferred_element_type=jnp.float32
    ).astype(jnp.bfloat16)
    grad_input = lax.all_to_all(share, "dp", split_axis=0, concat_axis=1, tiled=True)
    return (attention_output, query_gradient, key_gradient, grad_input, grad_weight)


def solution(mesh):
    in_specs = (
        P(("dp", "fsdp"), None),
        P(("dp", "fsdp"), None),
        P(("dp", "fsdp"), None),
        P(("dp", "fsdp"), None),
        P(("dp", "fsdp"), None),
        P(("dp", "fsdp"), None),
        P("fsdp", None),
        P(("dp", "fsdp"), None),
    )
    out_specs = (
        P(("dp", "fsdp"), None),
        P(("dp", "fsdp"), None),
        P(("dp", "fsdp"), None),
        P(("dp", "fsdp"), None),
        P(("dp", "fsdp"), None),
    )
    return jax.shard_map(local, mesh=mesh, in_specs=in_specs, out_specs=out_specs, check_vma=False)
```

profile of v0, /device:TPU:0, one launch (start us, length us, event | category | flops | bytes accessed | tf_op | source)
XLA Modules:
  0.0 167.1 jit_solution(17855206566767428514)
XLA Ops:
  7.2 0.0 copy-start
  7.2 0.0 all-gather.7.cloned.1.call-start
  7.2 0.8 add_bitcast_fusion
  8.1 10.3 %all-gather.1 = s32[8,3,8]{2,1,0:T(4,128)S(1)} all-gather(s32[1,3,8]{2,1,0:T(4,128)S(1)} %add_bitcast_fusion), channel_id=2, replica_groups=mesh['dp'=8,'fsdp'=4] {'dp'}, dimensions={0}, use_global_device_ids=true | all-gather | bytes 864 | tf_op jit(solution)/shard_map/all_gather | solution.py:92
  18.4 0.1 select_reduce_fusion.3
  18.6 0.1 select_reduce_fusion.2
  18.7 0.1 fusion.19
  18.8 0.9 reshape.70
  19.7 0.1 copy.113
  19.9 2.3 %copy.127 = bf16[128,4096]{0,1:T(8,128)(2,1)} copy(bf16[128,4096]{1,0:T(8,128)(2,1)} %param.12) | data formatting | bytes 2097152 | tf_op jit(solution)/shard_map/reshape | solution.py:16
  22.2 1.6 copy.128
  23.8 3.4 %fusion.31 = (f32[4,8,128]{2,1,0:T(8,128)S(1)}, f32[4,8,128,128]{2,3,1,0:T(8,128)}) fusion(pred[128,128]{0,1:T(8,128)(4,1)S(1)} %fusion.19, bf16[128,4,128,1]{0,2,3,1:T(8,128)(2,1)S(1)} %copy.113, bf16[128,4,8,128]{0,3,2,1:T(8,128)(2,1)} %bitcast.113), kind=kOutput, calls=%fused_computation.59 | convolution fusion | flops 136315008 | bytes 3309568 | tf_op jit(solution)/shard_map/sub | solution.py:30
  27.2 0.0 copy-start.3
  27.2 2.7 %fusion.10 = bf16[4,128,128]{1,2,0:T(8,128)(2,1)} fusion(bf16[128,4,8,128]{0,3,2,1:T(8,128)(2,1)S(1)} %bitcast.108, f32[4,8,128,128]{2,3,1,0:T(8,128)} %get-tuple-element.38, f32[4,8,128]{2,1,0:T(8,128)S(1)} %get-tuple-element.37), kind=kOutput, calls=%fused_computation.21 | convolution fusion | flops 135331840 | bytes 3293184 | tf_op jit(solution)/shard_map/lbjm,jlbw->mlw/dot_general | solution.py:42
  29.9 0.0 copy-done.3
  29.9 0.0 all-gather.7.cloned.1.call-update
  30.0 4.1 %copy.90 = bf16[128,8192]{0,1:T(8,128)(2,1)} copy(bf16[128,8192]{1,0:T(8,128)(2,1)} %param.8) | data formatting | bytes 4194304 | tf_op args[0]
  34.0 4.4 %all-to-all-start = ((bf16[128,8,1024]{0,2,1:T(8,128)(2,1)}), bf16[128,8,1024]{0,2,1:T(8,128)(2,1)}, u32[]{:S(2)}, u32[]{:S(2)}) async-start(bf16[128,8,1024]{0,2,1:T(8,128)(2,1)} %bitcast.107), calls=%async_computation | async-start | bytes 4194304 | tf_op jit(solution)/shard_map/all_to_all | solution.py:93
  38.4 0.0 all-gather.5.cloned.1.call-start
  38.5 0.0 copy-done
  38.5 0.7 collective-permute-start
  39.2 0.0 collective-permute-done
  39.2 0.0 copy-start.2
  39.2 0.7 copy-done.2
  39.9 0.0 all-gather.5.cloned.1.call-update
  39.9 0.0 reduce-scatter.2.cloned.1.call-start
  40.0 0.2 select_reduce_fusion.1
  40.2 0.1 select_reduce_fusion
  40.3 30.3 %all-to-all-done = bf16[128,8,1024]{0,2,1:T(8,128)(2,1)} async-done(((bf16[128,8,1024]{0,2,1:T(8,128)(2,1)}), bf16[128,8,1024]{0,2,1:T(8,128)(2,1)}, u32[]{:S(2)}, u32[]{:S(2)}) %all-to-all-start) | async-done | bytes 2097184 | tf_op jit(solution)/shard_map/all_to_all | solution.py:93
  70.7 3.9 %copy.91 = bf16[8,128,1024]{2,1,0:T(8,128)(2,1)} copy(bf16[8,128,1024]{1,2,0:T(8,128)(2,1)} %bitcast.7) | data formatting | bytes 4194304 | tf_op jit(solution)/shard_map/all_to_all | solution.py:93
  74.6 5.3 %fusion.7 = bf16[1024,1024]{1,0:T(8,128)(2,1)} fusion(bf16[1024,1024]{1,0:T(8,128)(2,1)} %bitcast.112, s32[1024]{0:T(1024)S(1)} %bitcast.130), kind=kOutput, calls=%fused_computation.12 | convolution fusion | flops 2149580800 | bytes 4198400 | tf_op jit(solution)/shard_map/dot_general | solution.py:101
  79.8 0.0 all-gather.7.cloned.1.call-done
  79.8 4.5 %fusion.33 = f32[1024,512]{1,0:T(8,128)} fusion(bf16[1024,1024]{1,0:T(8,128)(2,1)} %fusion.7, bf16[1024,512]{0,1:T(8,128)(2,1)} %all-gather.7.cloned.1.call-done), kind=kOutput, calls=%fused_computation.61 | convolution fusion | flops 1073741824 | bytes 5242880 | tf_op jit(solution)/shard_map/dot_general | solution.py:116
  84.4 0.0 reduce-scatter.2.cloned.1.call-update
  84.4 16.3 %all-gather.5.cloned.1.call-done = bf16[1024,512]{1,0:T(8,128)(2,1)} async-done(((bf16[256,512]{1,0:T(8,128)(2,1)}), bf16[1024,512]{1,0:T(8,128)(2,1)}) %all-gather.5.cloned.1.call-update) | async-done | bytes 1048592 | tf_op jit(solution)/shard_map/all_gather | solution.py:98
  100.7 4.1 %convolution_convert_fusion.3 = bf16[1024,512]{1,0:T(8,128)(2,1)} fusion(bf16[1024,1024]{1,0:T(8,128)(2,1)} %fusion.7, bf16[1024,512]{1,0:T(8,128)(2,1)} %all-gather.5.cloned.1.call-done), kind=kOutput, calls=%fused_computation.17 | convolution fusion | flops 1074266112 | bytes 4194304 | tf_op jit(solution)/shard_map/dot_general | solution.py:102
  104.7 4.2 %all-to-all-start.1 = ((bf16[8,128,512]{2,1,0:T(8,128)(2,1)}), bf16[8,128,512]{2,1,0:T(8,128)(2,1)}, u32[]{:S(2)}, u32[]{:S(2)}) async-start(bf16[8,128,512]{2,1,0:T(8,128)(2,1)} %bitcast.115), calls=%async_computation.1 | async-start | bytes 2097152 | tf_op jit(solution)/shard_map/all_to_all | solution.py:103
  109.0 4.2 %convolution_convert_fusion = bf16[1024,1024]{1,0:T(8,128)(2,1)} fusion(bf16[1024,512]{0,1:T(8,128)(2,1)} %all-gather.7.cloned.1.call-done, bf16[1024,512]{1,0:T(8,128)(2,1)} %all-gather.5.cloned.1.call-done), kind=kOutput, calls=%fused_computation.13 | convolution fusion | flops 1074790400 | bytes 4194304 | tf_op jit(solution)/shard_map/dot_general | solution.py:124
  113.2 11.2 %all-to-all-done.1 = bf16[8,128,512]{2,1,0:T(8,128)(2,1)} async-done(((bf16[8,128,512]{2,1,0:T(8,128)(2,1)}), bf16[8,128,512]{2,1,0:T(8,128)(2,1)}, u32[]{:S(2)}, u32[]{:S(2)}) %all-to-all-start.1) | async-done | bytes 1048608 | tf_op jit(solution)/shard_map/all_to_all | solution.py:103
  124.4 0.0 copy-start.4
  124.4 4.7 %all-to-all-start.2 = ((bf16[8,128,1024]{2,1,0:T(8,128)(2,1)}), bf16[8,128,1024]{2,1,0:T(8,128)(2,1)}, u32[]{:S(2)}, u32[]{:S(2)}) async-start(bf16[8,128,1024]{2,1,0:T(8,128)(2,1)} %bitcast.110), calls=%async_computation.2 | async-start | bytes 4194304 | tf_op jit(solution)/shard_map/all_to_all | solution.py:127
  129.1 1.4 reduce_sum.80
  130.5 0.1 copy.92
  130.6 0.0 copy-done.4
  130.6 3.0 %convolution_convert_fusion.2 = bf16[4,128,8,128]{3,1,2,0:T(8,128)(2,1)} fusion(bf16[128,4,128,1]{0,2,3,1:T(8,128)(2,1)S(1)} %bitcast.118, f32[4,8,128,128]{2,3,1,0:T(8,128)} %get-tuple-element.38, f32[4,8,128]{2,1,0:T(8,128)S(1)} %copy-done.4), kind=kOutput, calls=%fused_computation.16 | convolution fusion | flops 135790592 | bytes 3293184 | tf_op jit(solution)/shard_map/yxmd,dya->myxa/dot_general | solution.py:33
  133.6 2.3 %copy.105 = bf16[128,4096]{1,0:T(8,128)(2,1)} copy(bf16[128,4096]{0,1:T(8,128)(2,1)} %bitcast.117) | data formatting | bytes 2097152
  135.9 1.8 %fusion.32 = f32[4,128,128,8]{2,1,3,0:T(8,128)} fusion(bf16[128,4,128,1]{0,2,3,1:T(8,128)(2,1)S(1)} %bitcast.119, bf16[128,4,8,128]{0,3,2,1:T(8,128)(2,1)S(1)} %bitcast.109), kind=kOutput, calls=%fused_computation.60 | convolution fusion | flops 134217728 | bytes 3276800 | tf_op jit(solution)/shard_map/euaz,nuz->uaen/dot_general | solution.py:39
  137.7 5.4 %convolution_convert_fusion.1 = bf16[4,8,128,128]{2,3,1,0:T(8,128)(2,1)} fusion(bf16[128,4,128,1]{0,2,3,1:T(8,128)(2,1)S(1)} %copy.113, f32[4,128,128,8]{2,1,3,0:T(8,128)} %fusion.32, f32[4,8,128,128]{2,3,1,0:T(8,128)} %get-tuple-element.38, f32[4,8,128]{2,1,0:T(8,128)S(1)} %copy-done.4), kind=kOutput, calls=%fused_computation.15 | convolution fusion | flops 138416256 | bytes 5390336 | tf_op jit(solution)/shard_map/yxmd,dya->myxa/dot_general | solution.py:50
  143.1 0.0 copy-start.1
  143.1 2.4 %copy.106 = bf16[128,4096]{1,0:T(8,128)(2,1)} copy(bf16[128,4096]{0,1:T(8,128)(2,1)} %bitcast.116) | data formatting | bytes 2097152
  145.4 0.0 copy-done.1
  145.4 4.4 %fusion.9 = bf16[4,128,128]{1,2,0:T(8,128)(2,1)S(1)} fusion(bf16[128,4,8,128]{0,3,2,1:T(8,128)(2,1)S(1)} %bitcast.114, f32[4,128,128,8]{2,1,3,0:T(8,128)} %fusion.32, f32[4,8,128,128]{2,3,1,0:T(8,128)} %get-tuple-element.38, f32[4,8,128]{2,1,0:T(8,128)S(1)} %copy-done.4), kind=kOutput, calls=%fused_computation.20 | convolution fusion | flops 137957504 | bytes 5390336 | tf_op jit(solution)/shard_map/lbjm,jlbw->mlw/dot_general | solution.py:53
  149.8 0.8 copy.107
  150.6 5.0 %all-to-all-done.2 = bf16[8,128,1024]{2,1,0:T(8,128)(2,1)} async-done(((bf16[8,128,1024]{2,1,0:T(8,128)(2,1)}), bf16[8,128,1024]{2,1,0:T(8,128)(2,1)}, u32[]{:S(2)}, u32[]{:S(2)}) %all-to-all-start.2) | async-done | bytes 2097184 | tf_op jit(solution)/shard_map/all_to_all | solution.py:127
  155.6 3.1 %copy.129 = bf16[8,16,8,1024]{3,2,0,1:T(8,128)(2,1)} copy(bf16[8,16,8,1024]{3,2,1,0:T(8,128)(2,1)} %bitcast.49) | data formatting | bytes 4194304 | tf_op jit(solution)/shard_map/all_to_all | solution.py:127
  158.7 0.0 reduce-scatter.2.cloned.1.call-done
  158.7 1.9 %broadcast_multiply_fusion = f32[256,512]{1,0:T(8,128)} fusion(f32[256,512]{1,0:T(8,128)} %reduce-scatter.2.cloned.1.call-done), kind=kLoop, calls=%fused_computation.29 | loop fusion | flops 131072 | bytes 1048576 | tf_op jit(solution)/shard_map/mul | solution.py:123
  (5 shorter events, 0.1 us)
Async XLA Ops:
  7.2 31.3 %copy-start = (bf16[2048,512]{1,0:T(8,128)(2,1)S(1)}, bf16[2048,512]{1,0:T(8,128)(2,1)}, u32[]{:S(2)}) copy-start(bf16[2048,512]{1,0:T(8,128)(2,1)} %param.14) | copy-start | bytes 6291460
  7.2 72.7 %all-gather.7.cloned.1.call-start = ((), (), s32[]{:S(2)}) async-start(), calls=%async_computation.5 | async-start | bytes 1179648 | tf_op jit(solution)/shard_map/all_gather | solution.py:114
  27.2 2.7 %copy-start.3 = (f32[4,8,128]{2,1,0:T(8,128)}, f32[4,8,128]{2,1,0:T(8,128)S(1)}, u32[]{:S(2)}) copy-start(f32[4,8,128]{2,1,0:T(8,128)S(1)} %get-tuple-element.37) | copy-start | bytes 49156
  34.0 36.6 %all-to-all-start = ((bf16[128,8,1024]{0,2,1:T(8,128)(2,1)}), bf16[128,8,1024]{0,2,1:T(8,128)(2,1)}, u32[]{:S(2)}, u32[]{:S(2)}) async-start(bf16[128,8,1024]{0,2,1:T(8,128)(2,1)} %bitcast.107), calls=%async_computation | async-start | bytes 4194304 | tf_op jit(solution)/shard_map/all_to_all | solution.py:93
  38.4 62.2 %all-gather.5.cloned.1.call-start = ((), (), s32[]{:S(2)}) async-start(), calls=%async_computation.4 | async-start | bytes 1310720 | tf_op jit(solution)/shard_map/all_gather | solution.py:98
  38.5 0.7 collective-permute-start
  39.2 0.7 copy-start.2
  39.9 118.8 %reduce-scatter.2.cloned.1.call-start = ((), (), s32[]{:S(2)}) async-start(), calls=%async_computation.6 | async-start | bytes 2621440 | tf_op jit(solution)/shard_map/reduce_scatter | solution.py:115
  104.7 19.7 %all-to-all-start.1 = ((bf16[8,128,512]{2,1,0:T(8,128)(2,1)}), bf16[8,128,512]{2,1,0:T(8,128)(2,1)}, u32[]{:S(2)}, u32[]{:S(2)}) async-start(bf16[8,128,512]{2,1,0:T(8,128)(2,1)} %bitcast.115), calls=%async_computation.1 | async-start | bytes 2097152 | tf_op jit(solution)/shard_map/all_to_all | solution.py:103
  124.4 6.2 %copy-start.4 = (f32[4,8,128]{2,1,0:T(8,128)S(1)}, f32[4,8,128]{2,1,0:T(8,128)}, u32[]{:S(2)}) copy-start(f32[4,8,128]{2,1,0:T(8,128)} %copy-done.3) | copy-start | bytes 49156
  124.4 31.2 %all-to-all-start.2 = ((bf16[8,128,1024]{2,1,0:T(8,128)(2,1)}), bf16[8,128,1024]{2,1,0:T(8,128)(2,1)}, u32[]{:S(2)}, u32[]{:S(2)}) async-start(bf16[8,128,1024]{2,1,0:T(8,128)(2,1)} %bitcast.110), calls=%async_computation.2 | async-start | bytes 4194304 | tf_op jit(solution)/shard_map/all_to_all | solution.py:127
  143.1 2.4 %copy-start.1 = (bf16[128,4096]{0,1:T(8,128)(2,1)S(1)}, bf16[128,4096]{0,1:T(8,128)(2,1)}, u32[]{:S(2)}) copy-start(bf16[128,4096]{0,1:T(8,128)(2,1)} %copy.127) | copy-start | bytes 3145732
Sparse Core Ops, SparseCore 0:
  30.1 37.2 all-gather.6
  69.5 31.0 all-gather.4
  103.0 43.3 reduce-scatter.1
where the time goes:
time: 168 us; the launch traced here: 167 us
  waiting for transfers between devices  62.9 us (37%)
  matrix products  38.7 us (23%)
  local copies, waits for them, and re-layouts  22.4 us (13%)
  starting transfers between devices  14.1 us (8%)
  between operations  13.9 us (8%)
  blocking collectives  10.3 us (6%)
  other arithmetic  4.77 us (3%)
    all_to_all x1, waiting for transfers between devices, local(): lax.all_to_all(rollout_rows, 'dp', split_axis=1, concat_axis=0, tiled=True)  30.3 us
    all_gather x1, waiting for transfers between devices, local(): weight = lax.all_gather(piece, 'fsdp', axis=0, tiled=True)  16.3 us
    all_to_all x1, waiting for transfers between devices, local(): lax.all_to_all(partial.reshape(n_dp, tok_rows, partial.shape[1]), 'dp', s...  11.2 us
    all_gather x1, blocking collectives, local(): lax.all_gather(jnp.concatenate([lengths, dest, offset], axis=0), 'dp', ax...  10.3 us
    unnamed x14, local copies, waits for them, and re-layouts  10.2 us
    dot_general x1, matrix products, attend(): jnp.einsum('yxmd,dya->myxa', gradient_scores, heads_keys, preferred_eleme...  5.38 us
    dot_general x1, matrix products, local(): jnp.dot(pick, shared, preferred_element_type=jnp.float32)  5.25 us
    all_to_all x1, waiting for transfers between devices, local(): lax.all_to_all(share, 'dp', split_axis=0, concat_axis=1, tiled=True)  5 us
  transfers between devices with their start and end apart: 7, of which 4 were waited for; matrix products, arithmetic and copies ran while one was open for 31% of the time, Pallas kernels for 0%

commit v1 on v0

--- a/solution.py
+++ b/solution.py
@@ -7,6 +7,12 @@
 HEAD_SIZE = 128
 QUERY_HEADS = 32
 KEY_VALUE_HEADS = 4
+
+
+def laid_out(tiles, dim):
+    shape = list(tiles.shape[1:])
+    shape[dim] *= tiles.shape[0]
+    return jnp.moveaxis(tiles, 0, dim).reshape(shape)
 
 
 def attend(block_queries, block_keys, block_values, segment, gradient_block):
@@ -95,7 +101,19 @@
     piece = lax.dynamic_slice_in_dim(value_weight, me * block, block, axis=0)
     pairs = [(a * n_fsdp + b, b * n_dp + a) for a in range(n_dp) for b in range(n_fsdp)]
     piece = lax.ppermute(piece, ("dp", "fsdp"), pairs)
-    weight = lax.all_gather(piece, "fsdp", axis=0, tiled=True)
+    peers = lax.axis_size("fsdp")
+    pairs_2 = [(i, (i + 1) % peers) for i in range(peers)]
+    back = [(b_2, a_2) for a_2, b_2 in pairs_2]
+    lower, upper = ([], [])
+    for lap in range(peers - 1):
+        if lap % 2 == 0:
+            lower.append(lax.ppermute(lower[-1] if lower else piece, "fsdp", pairs_2))
+        else:
+            upper.append(lax.ppermute(upper[-1] if upper else piece, "fsdp", back))
+    blocks = jnp.stack([*lower[::-1], piece, *upper])
+    shift = lax.axis_index("fsdp") - len(lower)
+    blocks = blocks[(jnp.arange(peers) - shift) % peers]
+    weight = laid_out(blocks, 0)
     landing = tables(plan, tok_rows)
     pick = (jnp.arange(column, dtype=jnp.int32)[:, None] == landing[None, :]).astype(jnp.bfloat16)
     rows = jnp.dot(pick, shared, preferred_element_type=jnp.float32).astype(jnp.bfloat16)

time: 168 us -> 225 us (1.34)
  starting transfers between devices: 14.1 us -> 61.4 us
  blocking collectives: 10.3 us -> 29.6 us
  waiting for transfers between devices: 62.9 us -> 50.7 us
    ppermute x0 -> x3, starting transfers between devices: none -> 44.2 us  [the longest x2 40.1 us: local(): lower.append(lax.ppermute(lower[-1] if lower else piece, 'fsdp', pairs_2))]
    all_to_all x1, waiting for transfers between devices: 30.3 us -> 0.01 us  [local(): lax.all_to_all(rollout_rows, 'dp', split_axis=1, concat_axis=0, tiled=True)]
    all_gather x1, blocking collectives: 10.3 us -> 29.6 us  [local(): lax.all_gather(jnp.concatenate([lengths, dest, offset], axis=0), 'dp', ax...]
    ppermute x0 -> x3, waiting for transfers between devices: none -> 19.3 us  [the longest x2 14.9 us: local(): lower.append(lax.ppermute(lower[-1] if lower else piece, 'fsdp', pairs_2))]
    all_gather x1 -> x0, waiting for transfers between devices: 16.3 us -> none  [local(): weight = lax.all_gather(piece, 'fsdp', axis=0, tiled=True)]
    all_gather x1, waiting for transfers between devices: 0.01 us -> 15 us  [local(): gathered = lax.all_gather(value_gradient, 'dp', axis=0, tiled=True)]
    gather x0 -> x1, local copies, waits for them, and re-layouts: none -> 2.81 us  [local(): blocks = blocks[(jnp.arange(peers) - shift) % peers]]
    unnamed x14 -> x24, local copies, waits for them, and re-layouts: 10.2 us -> 9.65 us
  transfers between devices with their start and end apart: 7 -> 9, of which waited for: 4 -> 6; matrix products, arithmetic and copies ran while one was open for 31% -> 26% of each run, Pallas kernels for 0% -> 0%
where the time goes in v1:
time: 225 us; the launch traced here: 224 us
  starting transfers between devices  61.4 us (27%)
  waiting for transfers between devices  50.7 us (23%)
  matrix products  38.5 us (17%)
  blocking collectives  29.6 us (13%)
  local copies, waits for them, and re-layouts  22.8 us (10%)
  between operations  14.3 us (6%)
  other arithmetic  6.76 us (3%)
    ppermute x2, starting transfers between devices, local(): lower.append(lax.ppermute(lower[-1] if lower else piece, 'fsdp', pairs_2))  40.1 us
    all_gather x1, blocking collectives, local(): lax.all_gather(jnp.concatenate([lengths, dest, offset], axis=0), 'dp', ax...  29.6 us
    all_gather x1, waiting for transfers between devices, local(): gathered = lax.all_gather(value_gradient, 'dp', axis=0, tiled=True)  15 us
    ppermute x2, waiting for transfers between devices, local(): lower.append(lax.ppermute(lower[-1] if lower else piece, 'fsdp', pairs_2))  14.9 us
    all_to_all x1, waiting for transfers between devices, local(): lax.all_to_all(partial.reshape(n_dp, tok_rows, partial.shape[1]), 'dp', s...  11.3 us
    unnamed x24, local copies, waits for them, and re-layouts  9.65 us
    all_to_all x1, starting transfers between devices, local(): lax.all_to_all(partial.reshape(n_dp, tok_rows, partial.shape[1]), 'dp', s...  6.47 us
    dot_general x1, matrix products, attend(): jnp.einsum('yxmd,dya->myxa', gradient_scores, heads_keys, preferred_eleme...  5.36 us
  transfers between devices with their start and end apart: 9, of which 6 were waited for; matrix products, arithmetic and copies ran while one was open for 26% of the time, Pallas kernels for 0%

profile of v1, /device:TPU:0, one launch (start us, length us, event | category | flops | bytes accessed | tf_op | source)
XLA Modules:
  0.0 224.1 jit_solution(5446921550400279186)
XLA Ops:
  7.2 0.0 copy-start
  7.2 4.2 %copy.90 = bf16[128,8192]{0,1:T(8,128)(2,1)} copy(bf16[128,8192]{1,0:T(8,128)(2,1)} %param.8) | data formatting | bytes 4194304 | tf_op args[0]
  11.4 0.0 copy-start.5
  11.4 0.0 copy-start.6
  11.4 0.0 copy-start.1
  11.4 5.3 %all-to-all-start = ((bf16[128,8,1024]{0,2,1:T(8,128)(2,1)}), bf16[128,8,1024]{0,2,1:T(8,128)(2,1)}, u32[]{:S(2)}, u32[]{:S(2)}) async-start(bf16[128,8,1024]{0,2,1:T(8,128)(2,1)} %bitcast.114), calls=%async_computation | async-start | bytes 4194304 | tf_op jit(solution)/shard_map/all_to_all | solution.py:99
  16.7 0.0 all-gather.4.cloned.1.call-start
  16.8 0.0 copy-done.5
  16.8 0.0 copy-done.6
  16.8 0.0 copy-done.7
  16.8 29.6 %all-gather.1 = s32[8,3,8]{2,1,0:T(4,128)S(1)} all-gather(s32[1,3,8]{2,1,0:T(4,128)S(1)} %add_bitcast_fusion), channel_id=2, replica_groups=mesh['dp'=8,'fsdp'=4] {'dp'}, dimensions={0}, use_global_device_ids=true | all-gather | bytes 864 | tf_op jit(solution)/shard_map/all_gather | solution.py:98
  46.5 0.1 select_reduce_fusion.3
  46.6 0.1 select_reduce_fusion.2
  46.7 0.7 fusion.19
  47.4 0.0 copy-done.3
  47.5 0.0 copy-start.4
  47.5 0.1 copy.113
  47.6 0.0 copy-done.1
  47.6 1.4 copy.127
  49.0 0.0 copy-done.4
  49.0 3.4 %fusion.33 = (f32[4,8,128]{2,1,0:T(8,128)S(1)}, f32[4,8,128,128]{2,3,1,0:T(8,128)}) fusion(pred[128,128]{0,1:T(8,128)(4,1)S(1)} %copy-done.4, bf16[128,4,128,1]{0,2,3,1:T(8,128)(2,1)S(1)} %copy.113, bf16[128,4,8,128]{0,3,2,1:T(8,128)(2,1)} %bitcast.122), kind=kOutput, calls=%fused_computation.68 | convolution fusion | flops 136315008 | bytes 3309568 | tf_op jit(solution)/shard_map/sub | solution.py:36
  52.4 1.6 copy.128
  54.1 2.7 %fusion.10 = bf16[4,128,128]{1,2,0:T(8,128)(2,1)} fusion(bf16[128,4,8,128]{0,3,2,1:T(8,128)(2,1)S(1)} %bitcast.115, f32[4,8,128,128]{2,3,1,0:T(8,128)} %get-tuple-element.38, f32[4,8,128]{2,1,0:T(8,128)S(1)} %get-tuple-element.37), kind=kOutput, calls=%fused_computation.22 | convolution fusion | flops 135331840 | bytes 3293184 | tf_op jit(solution)/shard_map/lbjm,jlbw->mlw/dot_general | solution.py:48
  56.8 0.0 copy-done.8
  56.8 0.0 all-gather.4.cloned.1.call-update
  56.8 0.0 reduce-scatter.2.cloned.1.call-start
  56.8 0.2 select_reduce_fusion.1
  57.1 0.1 select_reduce_fusion
  57.2 0.0 all-to-all-done
  57.2 3.9 %copy.91 = bf16[8,128,1024]{2,1,0:T(8,128)(2,1)} copy(bf16[8,128,1024]{1,2,0:T(8,128)(2,1)} %bitcast.7) | data formatting | bytes 4194304 | tf_op jit(solution)/shard_map/all_to_all | solution.py:99
  61.1 5.3 %fusion.7 = bf16[1024,1024]{1,0:T(8,128)(2,1)} fusion(bf16[1024,1024]{1,0:T(8,128)(2,1)} %bitcast.119, s32[1024]{0:T(1024)S(1)} %bitcast.140), kind=kOutput, calls=%fused_computation.13 | convolution fusion | flops 2149580800 | bytes 4198400 | tf_op jit(solution)/shard_map/dot_general | solution.py:119
  66.4 15.0 %all-gather.4.cloned.1.call-done = bf16[1024,512]{0,1:T(8,128)(2,1)} async-done(((bf16[128,512]{0,1:T(8,128)(2,1)}), bf16[1024,512]{0,1:T(8,128)(2,1)}) %all-gather.4.cloned.1.call-update) | async-done | bytes 1048592 | tf_op jit(solution)/shard_map/all_gather | solution.py:132
  81.3 4.4 %fusion.35 = f32[1024,512]{1,0:T(8,128)} fusion(bf16[1024,1024]{1,0:T(8,128)(2,1)} %fusion.7, bf16[1024,512]{0,1:T(8,128)(2,1)} %all-gather.4.cloned.1.call-done), kind=kOutput, calls=%fused_computation.70 | convolution fusion | flops 1073741824 | bytes 5242880 | tf_op jit(solution)/shard_map/dot_general | solution.py:134
  85.8 0.0 reduce-scatter.2.cloned.1.call-update
  85.8 0.0 copy-done
  85.9 0.7 collective-permute-start
  86.5 0.0 collective-permute-done
  86.6 16.6 %collective-permute-start.1 = (bf16[256,512]{1,0:T(8,128)(2,1)S(1)}, bf16[256,512]{1,0:T(8,128)(2,1)}, u32[]{:S(2)}, u32[]{:S(2)}) collective-permute-start(bf16[256,512]{1,0:T(8,128)(2,1)S(1)} %collective-permute-done), channel_id=1, source_target_pairs={{0,1},{1,2},{2,3},{3,0},{4,5},{5,6},{6,7},{7,4},{8,9},{9,10},{10,1... | collective-permute-start | bytes 786440 | tf_op jit(solution)/shard_map/ppermute | solution.py:110
  103.2 4.1 %collective-permute-start.3 = (bf16[256,512]{1,0:T(8,128)(2,1)S(1)}, bf16[256,512]{1,0:T(8,128)(2,1)}, u32[]{:S(2)}, u32[]{:S(2)}) collective-permute-start(bf16[256,512]{1,0:T(8,128)(2,1)S(1)} %collective-permute-done), channel_id=1, source_target_pairs={{1,0},{2,1},{3,2},{0,3},{5,4},{6,5},{7,6},{4,7},{9,8},{10,9},{11,1... | collective-permute-start | bytes 786440 | tf_op jit(solution)/shard_map/ppermute | solution.py:112
  107.2 12.8 %collective-permute-done.1 = bf16[256,512]{1,0:T(8,128)(2,1)} collective-permute-done((bf16[256,512]{1,0:T(8,128)(2,1)S(1)}, bf16[256,512]{1,0:T(8,128)(2,1)}, u32[]{:S(2)}, u32[]{:S(2)}) %collective-permute-start.1) | collective-permute-done | bytes 262176 | tf_op jit(solution)/shard_map/ppermute | solution.py:110
  120.1 23.5 %collective-permute-start.2 = (bf16[256,512]{1,0:T(8,128)(2,1)}, bf16[256,512]{1,0:T(8,128)(2,1)}, u32[]{:S(2)}, u32[]{:S(2)}) collective-permute-start(bf16[256,512]{1,0:T(8,128)(2,1)} %collective-permute-done.1), channel_id=1, source_target_pairs={{0,1},{1,2},{2,3},{3,0},{4,5},{5,6},{6,7},{7,4},{8,9},{9,10},{10,1... | collective-permute-start | bytes 786440 | tf_op jit(solution)/shard_map/ppermute | solution.py:110
  143.6 4.4 %collective-permute-done.3 = bf16[256,512]{1,0:T(8,128)(2,1)} collective-permute-done((bf16[256,512]{1,0:T(8,128)(2,1)S(1)}, bf16[256,512]{1,0:T(8,128)(2,1)}, u32[]{:S(2)}, u32[]{:S(2)}) %collective-permute-start.3) | collective-permute-done | bytes 262176 | tf_op jit(solution)/shard_map/ppermute | solution.py:112
  148.0 2.0 collective-permute-done.2
  150.0 2.2 pad_maximum_fusion
  152.2 2.8 %gather_fusion = bf16[4,256,512]{2,1,0:T(8,128)(2,1)} fusion(bf16[4,256,512]{2,1,0:T(8,128)(2,1)} %pad_maximum_fusion, s32[1024]{0:T(1024)S(1)} %pad_clamp_fusion), kind=kCustom, calls=%fused_computation | custom fusion | bytes 2097168 | tf_op jit(solution)/shard_map/gather | solution.py:115
  155.0 4.1 %convolution_convert_fusion.3 = bf16[1024,512]{1,0:T(8,128)(2,1)} fusion(bf16[1024,1024]{1,0:T(8,128)(2,1)} %fusion.7, bf16[1024,512]{1,0:T(8,128)(2,1)} %bitcast.120), kind=kOutput, calls=%fused_computation.18 | convolution fusion | flops 1074266112 | bytes 4194304 | tf_op jit(solution)/shard_map/dot_general | solution.py:120
  159.1 6.5 %all-to-all-start.1 = ((bf16[8,128,512]{2,1,0:T(8,128)(2,1)}), bf16[8,128,512]{2,1,0:T(8,128)(2,1)}, u32[]{:S(2)}, u32[]{:S(2)}) async-start(bf16[8,128,512]{2,1,0:T(8,128)(2,1)} %bitcast.124), calls=%async_computation.1 | async-start | bytes 2097152 | tf_op jit(solution)/shard_map/all_to_all | solution.py:121
  165.6 4.2 %convolution_convert_fusion = bf16[1024,1024]{1,0:T(8,128)(2,1)} fusion(bf16[1024,512]{0,1:T(8,128)(2,1)} %all-gather.4.cloned.1.call-done, bf16[1024,512]{1,0:T(8,128)(2,1)} %bitcast.121), kind=kOutput, calls=%fused_computation.14 | convolution fusion | flops 1074790400 | bytes 4194304 | tf_op jit(solution)/shard_map/dot_general | solution.py:142
  169.7 11.3 %all-to-all-done.1 = bf16[8,128,512]{2,1,0:T(8,128)(2,1)} async-done(((bf16[8,128,512]{2,1,0:T(8,128)(2,1)}), bf16[8,128,512]{2,1,0:T(8,128)(2,1)}, u32[]{:S(2)}, u32[]{:S(2)}) %all-to-all-start.1) | async-done | bytes 1048608 | tf_op jit(solution)/shard_map/all_to_all | solution.py:121
  181.1 4.7 %all-to-all-start.2 = ((bf16[8,128,1024]{2,1,0:T(8,128)(2,1)}), bf16[8,128,1024]{2,1,0:T(8,128)(2,1)}, u32[]{:S(2)}, u32[]{:S(2)}) async-start(bf16[8,128,1024]{2,1,0:T(8,128)(2,1)} %bitcast.117), calls=%async_computation.2 | async-start | bytes 4194304 | tf_op jit(solution)/shard_map/all_to_all | solution.py:145
  185.8 1.4 reduce_sum.80
  187.1 0.1 copy.92
  187.3 0.0 copy-done.9
  187.3 3.0 %convolution_convert_fusion.2 = bf16[4,128,8,128]{3,1,2,0:T(8,128)(2,1)} fusion(bf16[128,4,128,1]{0,2,3,1:T(8,128)(2,1)S(1)} %bitcast.127, f32[4,8,128,128]{2,3,1,0:T(8,128)} %get-tuple-element.38, f32[4,8,128]{2,1,0:T(8,128)S(1)} %copy-done.9), kind=kOutput, calls=%fused_computation.17 | convolution fusion | flops 135790592 | bytes 3293184 | tf_op jit(solution)/shard_map/yxmd,dya->myxa/dot_general | solution.py:39
  190.3 2.3 %copy.105 = bf16[128,4096]{1,0:T(8,128)(2,1)} copy(bf16[128,4096]{0,1:T(8,128)(2,1)} %bitcast.126) | data formatting | bytes 2097152
  192.5 1.8 fusion.34
  194.3 5.4 %convolution_convert_fusion.1 = bf16[4,8,128,128]{2,3,1,0:T(8,128)(2,1)} fusion(bf16[128,4,128,1]{0,2,3,1:T(8,128)(2,1)S(1)} %copy.113, f32[4,128,128,8]{2,1,3,0:T(8,128)} %fusion.34, f32[4,8,128,128]{2,3,1,0:T(8,128)} %get-tuple-element.38, f32[4,8,128]{2,1,0:T(8,128)S(1)} %copy-done.9), kind=kOutput, calls=%fused_computation.16 | convolution fusion | flops 138416256 | bytes 5390336 | tf_op jit(solution)/shard_map/yxmd,dya->myxa/dot_general | solution.py:56
  199.7 2.4 %copy.106 = bf16[128,4096]{1,0:T(8,128)(2,1)} copy(bf16[128,4096]{0,1:T(8,128)(2,1)} %bitcast.125) | data formatting | bytes 2097152
  202.0 0.0 copy-done.2
  202.1 4.3 %fusion.9 = bf16[4,128,128]{1,2,0:T(8,128)(2,1)S(1)} fusion(bf16[128,4,8,128]{0,3,2,1:T(8,128)(2,1)S(1)} %bitcast.123, f32[4,128,128,8]{2,1,3,0:T(8,128)} %fusion.34, f32[4,8,128,128]{2,3,1,0:T(8,128)} %get-tuple-element.38, f32[4,8,128]{2,1,0:T(8,128)S(1)} %copy-done.9), kind=kOutput, calls=%fused_computation.21 | convolution fusion | flops 137957504 | bytes 5390336 | tf_op jit(solution)/shard_map/lbjm,jlbw->mlw/dot_general | solution.py:59
  206.4 0.8 copy.107
  207.1 5.1 %all-to-all-done.2 = bf16[8,128,1024]{2,1,0:T(8,128)(2,1)} async-done(((bf16[8,128,1024]{2,1,0:T(8,128)(2,1)}), bf16[8,128,1024]{2,1,0:T(8,128)(2,1)}, u32[]{:S(2)}, u32[]{:S(2)}) %all-to-all-start.2) | async-done | bytes 2097184 | tf_op jit(solution)/shard_map/all_to_all | solution.py:145
  212.2 3.1 %copy.129 = bf16[8,16,8,1024]{3,2,0,1:T(8,128)(2,1)} copy(bf16[8,16,8,1024]{3,2,1,0:T(8,128)(2,1)} %bitcast.55) | data formatting | bytes 4194304 | tf_op jit(solution)/shard_map/all_to_all | solution.py:145
  215.4 1.9 broadcast_multiply_fusion
  (15 shorter events, 0.1 us)
Async XLA Ops:
  7.2 78.7 %copy-start = (bf16[2048,512]{1,0:T(8,128)(2,1)S(1)}, bf16[2048,512]{1,0:T(8,128)(2,1)}, u32[]{:S(2)}) copy-start(bf16[2048,512]{1,0:T(8,128)(2,1)} %param.14) | copy-start | bytes 6291460
  11.4 5.4 %copy-start.5 = (s32[1,8]{1,0:T(1,128)S(1)}, s32[1,8]{1,0:T(1,128)}, u32[]{:S(2)}) copy-start(s32[1,8]{1,0:T(1,128)} %param.11) | copy-start | bytes 100
  11.4 5.4 %copy-start.6 = (s32[1,8]{1,0:T(1,128)S(1)}, s32[1,8]{1,0:T(1,128)}, u32[]{:S(2)}) copy-start(s32[1,8]{1,0:T(1,128)} %param.10) | copy-start | bytes 100
  11.4 5.4 %copy-start.7 = (s32[1,8]{1,0:T(1,128)S(1)}, s32[1,8]{1,0:T(1,128)}, u32[]{:S(2)}) copy-start(s32[1,8]{1,0:T(1,128)} %param.9) | copy-start | bytes 100
  11.4 36.0 %copy-start.3 = (bf16[128,512]{1,0:T(8,128)(2,1)S(1)}, bf16[128,512]{1,0:T(8,128)(2,1)}, u32[]{:S(2)}) copy-start(bf16[128,512]{1,0:T(8,128)(2,1)} %param.13) | copy-start | bytes 393220
  11.4 36.2 %copy-start.1 = (bf16[128,4096]{1,0:T(8,128)(2,1)S(1)}, bf16[128,4096]{1,0:T(8,128)(2,1)}, u32[]{:S(2)}) copy-start(bf16[128,4096]{1,0:T(8,128)(2,1)} %param.12) | copy-start | bytes 3145732
  11.4 45.8 %all-to-all-start = ((bf16[128,8,1024]{0,2,1:T(8,128)(2,1)}), bf16[128,8,1024]{0,2,1:T(8,128)(2,1)}, u32[]{:S(2)}, u32[]{:S(2)}) async-start(bf16[128,8,1024]{0,2,1:T(8,128)(2,1)} %bitcast.114), calls=%async_computation | async-start | bytes 4194304 | tf_op jit(solution)/shard_map/all_to_all | solution.py:99
  16.7 64.6 %all-gather.4.cloned.1.call-start = ((), (), s32[]{:S(2)}) async-start(), calls=%async_computation.4 | async-start | bytes 1179648 | tf_op jit(solution)/shard_map/all_gather | solution.py:132
  47.5 1.6 copy-start.4
  52.4 4.3 %copy-start.8 = (f32[4,8,128]{2,1,0:T(8,128)}, f32[4,8,128]{2,1,0:T(8,128)S(1)}, u32[]{:S(2)}) copy-start(f32[4,8,128]{2,1,0:T(8,128)S(1)} %get-tuple-element.37) | copy-start | bytes 49156
  56.8 158.6 %reduce-scatter.2.cloned.1.call-start = ((), (), s32[]{:S(2)}) async-start(), calls=%async_computation.5 | async-start | bytes 2621440 | tf_op jit(solution)/shard_map/reduce_scatter | solution.py:133
  85.9 0.7 collective-permute-start
  86.6 33.5 %collective-permute-start.1 = (bf16[256,512]{1,0:T(8,128)(2,1)S(1)}, bf16[256,512]{1,0:T(8,128)(2,1)}, u32[]{:S(2)}, u32[]{:S(2)}) collective-permute-start(bf16[256,512]{1,0:T(8,128)(2,1)S(1)} %collective-permute-done), channel_id=1, source_target_pairs={{0,1},{1,2},{2,3},{3,0},{4,5},{5,6},{6,7},{7,4},{8,9},{9,10},{10,1... | collective-permute-start | bytes 786440 | tf_op jit(solution)/shard_map/ppermute | solution.py:110
  103.2 44.8 %collective-permute-start.3 = (bf16[256,512]{1,0:T(8,128)(2,1)S(1)}, bf16[256,512]{1,0:T(8,128)(2,1)}, u32[]{:S(2)}, u32[]{:S(2)}) collective-permute-start(bf16[256,512]{1,0:T(8,128)(2,1)S(1)} %collective-permute-done), channel_id=1, source_target_pairs={{1,0},{2,1},{3,2},{0,3},{5,4},{6,5},{7,6},{4,7},{9,8},{10,9},{11,1... | collective-permute-start | bytes 786440 | tf_op jit(solution)/shard_map/ppermute | solution.py:112
  120.1 29.9 %collective-permute-start.2 = (bf16[256,512]{1,0:T(8,128)(2,1)}, bf16[256,512]{1,0:T(8,128)(2,1)}, u32[]{:S(2)}, u32[]{:S(2)}) collective-permute-start(bf16[256,512]{1,0:T(8,128)(2,1)} %collective-permute-done.1), channel_id=1, source_target_pairs={{0,1},{1,2},{2,3},{3,0},{4,5},{5,6},{6,7},{7,4},{8,9},{9,10},{10,1... | collective-permute-start | bytes 786440 | tf_op jit(solution)/shard_map/ppermute | solution.py:110
  159.1 22.0 %all-to-all-start.1 = ((bf16[8,128,512]{2,1,0:T(8,128)(2,1)}), bf16[8,128,512]{2,1,0:T(8,128)(2,1)}, u32[]{:S(2)}, u32[]{:S(2)}) async-start(bf16[8,128,512]{2,1,0:T(8,128)(2,1)} %bitcast.124), calls=%async_computation.1 | async-start | bytes 2097152 | tf_op jit(solution)/shard_map/all_to_all | solution.py:121
  181.1 6.2 %copy-start.9 = (f32[4,8,128]{2,1,0:T(8,128)S(1)}, f32[4,8,128]{2,1,0:T(8,128)}, u32[]{:S(2)}) copy-start(f32[4,8,128]{2,1,0:T(8,128)} %copy-done.8) | copy-start | bytes 49156
  181.1 31.1 %all-to-all-start.2 = ((bf16[8,128,1024]{2,1,0:T(8,128)(2,1)}), bf16[8,128,1024]{2,1,0:T(8,128)(2,1)}, u32[]{:S(2)}, u32[]{:S(2)}) async-start(bf16[8,128,1024]{2,1,0:T(8,128)(2,1)} %bitcast.117), calls=%async_computation.2 | async-start | bytes 4194304 | tf_op jit(solution)/shard_map/all_to_all | solution.py:145
  199.7 2.4 %copy-start.2 = (bf16[128,4096]{0,1:T(8,128)(2,1)S(1)}, bf16[128,4096]{0,1:T(8,128)(2,1)}, u32[]{:S(2)}) copy-start(bf16[128,4096]{0,1:T(8,128)(2,1)} %copy.127) | copy-start | bytes 3145732
Sparse Core Ops, SparseCore 0:
  56.9 24.3 all-gather.3
  85.9 66.3 reduce-scatter.1
